TPU v7x, 128 devices: a whole 4x4x4 slice. The times are simulated.
128 devices in a mesh: dp: 16 (over x, y_lo, core), tensor: 8 (over y_hi, z).
Axes of the slice: x: 4, y: 4 (y_hi: 2, y_lo: 2; y = y_hi * 2 + y_lo), z: 4, core: 2. Of those that a mesh axis runs over, the one named last changes fastest.
Arguments:
- prompt_keys: bfloat16 [128, 512, 1024], P('dp', None, 'tensor'), may hold values from -6 to 6
- prompt_values: bfloat16 [128, 512, 1024], P('dp', None, 'tensor'), may hold values from -6 to 6
- query_states: bfloat16 [128, 64, 8192], P('dp', None, 'tensor'), may hold values from -140 to 140
- query_keys: bfloat16 [128, 64, 1024], P('dp', None, 'tensor'), may hold values from -6 to 6
- query_values: bfloat16 [128, 64, 1024], P('dp', None, 'tensor'), may hold values from -6 to 6
- lengths: int32 [128], P('dp'), may hold values from 1 to 512, 32768 in all
- residual: bfloat16 [128, 64, 8192], P('dp', None, 'tensor'), may hold values from -6 to 6
- out_weight: bfloat16 [8192, 8192], P('tensor', 'dp'), may hold values from -0.0625 to 0.0625
- final_gain: float32 [8192], P('tensor'), may hold values from 0.25 to 1.75
- conn_weight: bfloat16 [8192, 3584], P('tensor'), may hold values from -0.0625 to 0.0625
- owner: int32 [16, 8], P('dp'), may hold values from 0 to 7, each once within a row
- latents: bfloat16 [128, 1024, 128], P(('dp', 'tensor')), may hold values from -6 to 6
- noise: bfloat16 [128, 1024, 128], P(('dp', 'tensor')), may hold values from -6 to 6
- timesteps: int32 [128], P(('dp', 'tensor')), may hold values from 0 to 999
- patch_weight: bfloat16 [128, 1792], replicated, may hold values from -0.5 to 0.5
- time_embedding: float32 [1792], replicated, may hold values from -4 to 4
- image_norm_gain: float32 [1792], replicated, may hold values from 0.25 to 1.75
- query_matrix: bfloat16 [1792, 1792], replicated, may hold values from -0.125 to 0.125
- velocity_head_weight: bfloat16 [1792, 128], replicated, may hold values from -0.125 to 0.125
Outputs:
- velocity: float32 [128, 1024, 128], P(('dp', 'tensor'))
- query_grad: float32 [1792, 1792], P(('dp', 'tensor'))
All inputs are finite; a program needn't handle non-finite values. No bound on the sum of `lengths` on one device may be relied on, other than what follows from the above.
Results may differ from a plain program's by a relative error of at most 0.025.
Values may be sent and summed in bfloat16 or wider, within the bound.
A program may use at most 128 MiB of HBM per device.

v0:
```python
import math

import jax
import jax.numpy as jnp
from jax import lax
from jax.sharding import PartitionSpec as P

D = 8192
HEAD = 128
NQ = 64
DHEAD = 112
NT = 1000


eps = 1e-06
grad_gain = 16.0


def llm_attend(queries, keys, values, own_keys, own_values, lens):
    prompts, rows, width = queries.shape
    klen = keys.shape[1]
    kv_count = keys.shape[2] // HEAD
    group = width // HEAD // kv_count
    scale = 1.0 / HEAD**0.5
    qr = queries.reshape(prompts, rows, kv_count, group, HEAD)
    kr = keys.reshape(prompts, klen, kv_count, HEAD)
    vr = values.reshape(prompts, klen, kv_count, HEAD)
    ok = own_keys.reshape(prompts, rows, kv_count, HEAD)
    ov = own_values.reshape(prompts, rows, kv_count, HEAD)
    first = jnp.einsum("pikgd,pjkd->pkgij", qr, kr, preferred_element_type=jnp.float32) * scale
    second = jnp.einsum("pikgd,pjkd->pkgij", qr, ok, preferred_element_type=jnp.float32) * scale
    valid = jnp.arange(klen)[None, :] < lens[:, None]
    first = jnp.where(valid[:, None, None, None, :], first, -jnp.inf)
    causal = jnp.arange(rows)[None, :] <= jnp.arange(rows)[:, None]
    second = jnp.where(causal[None, None, None], second, -jnp.inf)
    top = jnp.maximum(jnp.max(first, -1, keepdims=True), jnp.max(second, -1, keepdims=True))
    efirst = jnp.exp(first - top)
    esecond = jnp.exp(second - top)
    total = jnp.sum(efirst, -1, keepdims=True) + jnp.sum(esecond, -1, keepdims=True)
    pfirst = (efirst / total).astype(jnp.bfloat16)
    psecond = (esecond / total).astype(jnp.bfloat16)
    out = jnp.einsum("pkgij,pjkd->pikgd", pfirst, vr, preferred_element_type=jnp.float32)
    out = out + jnp.einsum("pkgij,pjkd->pikgd", psecond, ov, preferred_element_type=jnp.float32)
    return out.reshape(prompts, rows, width).astype(jnp.bfloat16)


def flow_matching_step(
    condition_rows,
    latents,
    noise,
    step_count,
    patch_weight,
    time_embedding,
    image_norm_gain,
    query_matrix,
    velocity_head_weight,
    count_of_rows,
):
    images, tokens, patch = latents.shape
    width = query_matrix.shape[0]
    heads = width // DHEAD
    scale = 1.0 / DHEAD**0.5
    tval = ((step_count.astype(jnp.float32) + 0.5) / NT)[:, None, None]
    noisy = ((1.0 - tval) * latents.astype(jnp.float32) + tval * noise.astype(jnp.float32)).astype(
        jnp.bfloat16
    )
    hidden = jnp.dot(
        noisy.reshape(-1, patch), patch_weight, preferred_element_type=jnp.float32
    ).reshape(images, tokens, width)
    hidden = hidden + tval * time_embedding
    normed = (
        hidden * lax.rsqrt(jnp.mean(hidden * hidden, -1, keepdims=True) + eps) * image_norm_gain
    ).astype(jnp.bfloat16)
    normalized_rows = normed.reshape(-1, width)
    queries = jnp.dot(normalized_rows, query_matrix, preferred_element_type=jnp.float32).astype(
        jnp.bfloat16
    )
    queries = queries.reshape(images, tokens, heads, DHEAD)
    keys = condition_rows[:, :, :width].reshape(images, -1, heads, DHEAD)
    vals = condition_rows[:, :, width:].reshape(images, -1, heads, DHEAD)
    scores = (
        jnp.einsum("itnd,ijnd->intj", queries, keys, preferred_element_type=jnp.float32) * scale
    )
    expo = jnp.exp(scores)
    probs = expo / jnp.sum(expo, -1, keepdims=True)
    attn = jnp.einsum(
        "intj,ijnd->itnd", probs.astype(jnp.bfloat16), vals, preferred_element_type=jnp.float32
    )
    attn = attn.reshape(images, tokens, width).astype(jnp.bfloat16)
    mixed = (hidden + attn.astype(jnp.float32)).astype(jnp.bfloat16)
    velocity = jnp.dot(
        mixed.reshape(-1, width), velocity_head_weight, preferred_element_type=jnp.float32
    ).reshape(images, tokens, patch)
    target = noise.astype(jnp.float32) - latents.astype(jnp.float32)
    dvel = ((velocity - target) * (grad_gain / math.sqrt(count_of_rows))).astype(jnp.bfloat16)
    dmixed = lax.dot_general(
        dvel.reshape(-1, patch),
        velocity_head_weight,
        (((1,), (1,)), ((), ())),
        preferred_element_type=jnp.float32,
    )
    dmixed = dmixed.astype(jnp.bfloat16).reshape(images, tokens, heads, DHEAD)
    dprob = jnp.einsum("itnd,ijnd->intj", dmixed, vals, preferred_element_type=jnp.float32)
    dscore = (probs * (dprob - jnp.sum(probs * dprob, -1, keepdims=True)) * scale).astype(
        jnp.bfloat16
    )
    query_gradient = jnp.einsum("intj,ijnd->itnd", dscore, keys, preferred_element_type=jnp.float32)
    query_gradient = query_gradient.reshape(-1, width).astype(jnp.bfloat16)
    return (velocity, normalized_rows, query_gradient)


def on_device(
    prompt_keys,
    prompt_values,
    query_states,
    query_keys,
    query_values,
    lengths,
    residual,
    out_weight,
    final_gain,
    conn_weight,
    owner,
    latents,
    noise,
    timesteps,
    patch_weight,
    time_embedding,
    image_norm_gain,
    query_matrix,
    velocity_head_weight,
):
    per_group = query_states.shape[0]
    local_rows = per_group * NQ
    img_dev = latents.shape[0]
    count_of_rows = img_dev * lax.axis_size("dp") * lax.axis_size("tensor") * latents.shape[1]
    attended = llm_attend(
        query_states, prompt_keys, prompt_values, query_keys, query_values, lengths
    ).reshape(local_rows, -1)
    partial_value = jnp.dot(
        attended,
        lax.all_gather(out_weight, "dp", axis=1, tiled=True),
        preferred_element_type=jnp.float32,
    ).astype(jnp.bfloat16)
    summed = lax.psum_scatter(partial_value, "tensor", scatter_dimension=1, tiled=True).astype(
        jnp.float32
    )
    llm_out = residual.reshape(local_rows, -1).astype(jnp.float32) + summed
    squares = jnp.sum(llm_out * llm_out, -1).reshape(per_group, NQ)
    scaled = (llm_out * final_gain).astype(jnp.bfloat16)
    parts = jnp.dot(scaled, conn_weight, preferred_element_type=jnp.float32).astype(jnp.bfloat16)
    parts = parts.reshape(per_group, NQ, -1)
    order = owner[0]
    moved = jnp.take(parts, order, axis=0)
    moved_squares = jnp.take(squares, order, axis=0)
    totals = lax.psum(moved_squares, "tensor")
    mine = lax.dynamic_slice_in_dim(totals, lax.axis_index("tensor") * img_dev, img_dev, 0)
    cond_sum = lax.psum_scatter(moved, "tensor", scatter_dimension=0, tiled=True).astype(
        jnp.float32
    )
    stat = mine / D
    image_condition = (cond_sum * lax.rsqrt(stat + eps)[:, :, None]).astype(jnp.bfloat16)
    velocity, normalized_rows, query_gradient = flow_matching_step(
        image_condition,
        latents,
        noise,
        timesteps,
        patch_weight,
        time_embedding,
        image_norm_gain,
        query_matrix,
        velocity_head_weight,
        count_of_rows,
    )
    query_grad = lax.psum_scatter(
        lax.dot_general(
            normalized_rows,
            query_gradient,
            (((0,), (0,)), ((), ())),
            preferred_element_type=jnp.float32,
        ),
        ("dp", "tensor"),
        scatter_dimension=0,
        tiled=True,
    )
    return (velocity, query_grad)


def solution(mesh):
    return jax.shard_map(
        on_device,
        mesh=mesh,
        in_specs=(
            P("dp", None, "tensor"),
            P("dp", None, "tensor"),
            P("dp", None, "tensor"),
            P("dp", None, "tensor"),
            P("dp", None, "tensor"),
            P("dp"),
            P("dp", None, "tensor"),
            P("tensor", "dp"),
            P("tensor"),
            P("tensor", None),
            P("dp", None),
            P(("dp", "tensor"), None, None),
            P(("dp", "tensor"), None, None),
            P(("dp", "tensor")),
            P(),
            P(),
            P(),
            P(),
            P(),
        ),
        out_specs=(P(("dp", "tensor"), None, None), P(("dp", "tensor"), None)),
        check_vma=False,
    )
```

profile of v0, /device:TPU:17, one launch (start us, length us, event | category | flops | bytes accessed | tf_op | source)
XLA Modules:
  0.0 849.7 jit_solution(11915302980476101364)
XLA Ops:
  7.2 0.0 all-gather.2.cloned.1.call-start
  7.2 0.7 all-gather.2.cloned.1.call-update
  7.9 0.0 reduce-scatter.5.cloned.1.call-start
  8.0 0.7 iota_compare_fusion.1
  8.7 2.0 fusion.69
  10.8 1.3 bitcast_reduce_fusion
  12.1 0.5 fusion.22
  12.6 2.1 fusion.3
  14.8 3.4 fusion.4
  18.2 0.7 fusion.23
  18.9 0.7 copy.41
  19.6 84.1 %all-gather.2.cloned.1.call-done = bf16[1024,8192]{1,0:T(8,128)(2,1)} async-done(((bf16[1024,512]{1,0:T(8,128)(2,1)}), bf16[1024,8192]{1,0:T(8,128)(2,1)}) %all-gather.2.cloned.1.call-update) | async-done | bytes 16777232 | tf_op jit(solution)/shard_map/all_gather | solution.py:142
  103.7 16.8 %convolution_convert_fusion = bf16[512,8192]{1,0:T(8,128)(2,1)} fusion(bf16[1024,8192]{1,0:T(8,128)(2,1)} %all-gather.2.cloned.1.call-done, bf16[64,8,8,128]{3,2,1,0:T(8,128)(2,1)S(1)} %bitcast.138), kind=kOutput, calls=%fused_computation.3 | convolution fusion | flops 8594128896 | bytes 26214400 | tf_op jit(solution)/shard_map/dot_general | solution.py:140
  120.6 0.2 reduce-scatter.7.cloned.1.call-start
  120.8 0.4 copy-done.29
  121.3 111.4 %reduce-scatter.5.cloned.1.call-done = bf16[512,1024]{1,0:T(8,128)(2,1)} async-done(((bf16[512,8192]{1,0:T(8,128)(2,1)}), bf16[512,1024]{1,0:T(8,128)(2,1)}) %reduce-scatter.5.cloned.1.call-update) | async-done | bytes 1048592 | tf_op jit(solution)/shard_map/reduce_scatter | solution.py:145
  232.7 9.2 %convolution_convert_fusion.1 = bf16[512,3584]{1,0:T(8,128)(2,1)} fusion(bf16[1024,3584]{1,0:T(8,128)(2,1)} %param.28, bf16[512,1024]{1,0:T(8,128)(2,1)} %reduce-scatter.5.cloned.1.call-done, bf16[512,1024]{1,0:T(8,128)(2,1)S(1)} %bitcast.137, f32[1024]{0:T(1024)S(1)} %copy-done.28), kind=kOutput, calls=%fused_computation.13 | convolution fusion | flops 3762552832 | bytes 13111296 | tf_op jit(solution)/shard_map/dot_general | solution.py:151
  241.9 4.7 gather_fusion
  246.5 4.4 broadcast_select_fusion
  251.7 1.2 multiply_reduce_fusion
  252.9 2.9 copy-done.2
  255.7 11.4 %convolution_convert_fusion.2 = bf16[1024,1792]{1,0:T(8,128)(2,1)} fusion(bf16[1792,1792]{1,0:T(8,128)(2,1)} %param.36, f32[1024,1792]{1,0:T(8,128)S(1)} %get-tuple-element.9, f32[1792]{0:T(1024)S(1)} %copy-done.27, f32[1024]{0:T(1024)S(1)} %add_rsqrt_fusion, f32[1792]{0:T(1024)S(1)} %broadcast_multiply_fusion), kind=kOutput, calls=%fused_computation.21 | convolution fusion | flops 6585843712 | bytes 17451008 | tf_op jit(solution)/shard_map/dot_general | solution.py:75
  267.1 6.1 copy.42
  273.2 0.4 multiply_reduce_fusion.2
  273.6 0.1 reshape.275
  273.7 0.6 gather_fusion.1
  274.3 0.1 broadcast_select_fusion.1
  274.3 18.6 %psum.7 = f32[8,64]{1,0:T(8,128)S(1)} all-reduce(f32[8,64]{1,0:T(8,128)S(1)} %broadcast_select_fusion.1), channel_id=1, replica_groups=mesh['dp'=16,'tensor'=8] {'tensor'}, use_global_device_ids=true, to_apply=%region_7.8 | all-reduce | flops 512 | bytes 4096 | tf_op jit(solution)/shard_map/psum | solution.py:156
  293.0 37.8 %reduce-scatter.7.cloned.1.call-done = bf16[1,64,3584]{2,1,0:T(8,128)(2,1)} async-done(((bf16[8,64,3584]{2,1,0:T(8,128)(2,1)}), bf16[1,64,3584]{2,1,0:T(8,128)(2,1)}) %reduce-scatter.7.cloned.1.call-update) | async-done | bytes 458768 | tf_op jit(solution)/shard_map/reduce_scatter | solution.py:158
  330.7 1.2 multiply_convert_fusion.4
  331.9 0.4 reshape.278
  332.3 0.4 reshape.276
  332.7 3.3 fusion.9
  336.0 4.2 bitcast_convert_fusion
  340.2 8.5 copy.45
  348.7 6.3 fusion.24
  355.0 2.9 convolution_convert_fusion.3
  357.9 5.9 copy.46
  363.9 4.7 fusion.50
  368.6 10.5 %fusion.17 = bf16[16,112,1024]{2,1,0:T(8,128)(2,1)} fusion(f32[16,1024,64]{1,2,0:T(8,128)} %fusion.50, bf16[64,16,112]{2,1,0:T(8,128)(2,1)S(1)} %reshape.278, f32[16,1024,64]{1,2,0:T(8,128)} %copy-done.3, f32[16,1024]{1,0:T(8,128)S(1)} %get-tuple-element.10), kind=kOutput, calls=%fused_computation.30 | convolution fusion | flops 246169664 | bytes 12353536 | tf_op jit(solution)/shard_map/intj,ijnd->itnd/dot_general | solution.py:107
  379.0 13.5 %fusion.64 = f32[1792,1792]{1,0:T(8,128)} fusion(bf16[1024,1792]{0,1:T(8,128)(2,1)} %bitcast.139, f32[1024,1792]{1,0:T(8,128)} %copy-done.2, f32[1792]{0:T(1024)S(1)} %copy-done.27, f32[1024]{0:T(1024)S(1)} %add_rsqrt_fusion, f32[1792]{0:T(1024)S(1)} %broadcast_multiply_fusion), kind=kOutput, calls=%fused_computation.95 | convolution fusion | flops 6584008704 | bytes 23873536 | tf_op jit(solution)/shard_map/dot_general | solution.py:176
  392.6 349.9 %fusion = f32[16,1792]{1,0:T(8,128)S(1)} fusion(f32[1792,1792]{1,0:T(8,128)} %fusion.64), kind=kCustom, calls=%all-reduce-scatter | all-reduce-scatter fusion | flops 3670017 | bytes 12959744
  742.6 1.3 collective-permute-start.15
  743.9 1.9 collective-permute-start
  745.8 1.9 collective-permute-start.1
  747.7 1.9 collective-permute-start.10
  749.6 2.6 collective-permute-start.11
  752.3 6.5 collective-permute-start.12
  758.8 1.3 collective-permute-start.13
  760.2 11.4 %collective-permute-start.14 = (f32[16,1792]{1,0:T(8,128)S(1)}, f32[16,1792]{1,0:T(8,128)S(1)}, u32[]{:S(2)}, u32[]{:S(2)}) collective-permute-start(f32[16,1792]{1,0:T(8,128)S(1)} %fusion), channel_id=1, source_target_pairs={{0,15},{1,16},{2,17},{3,18},{4,19},{5,20},{6,21},{7,22},{8,23},{9,... | collective-permute-start | bytes 344072
  771.6 6.2 collective-permute-done.10
  777.8 1.9 collective-permute-start.2
  779.7 3.1 collective-permute-start.3
  782.9 3.8 collective-permute-start.4
  786.7 2.6 collective-permute-start.5
  789.3 9.9 %collective-permute-start.6 = (f32[16,1792]{1,0:T(8,128)S(1)}, f32[16,1792]{1,0:T(8,128)S(1)}, u32[]{:S(2)}, u32[]{:S(2)}) collective-permute-start(f32[16,1792]{1,0:T(8,128)S(1)} %fusion), channel_id=1, source_target_pairs={{0,7},{1,8},{2,9},{3,10},{4,11},{5,12},{6,13},{7,14},{8,15},{9,16}... | collective-permute-start | bytes 344072
  799.2 17.6 %collective-permute-start.7 = (f32[16,1792]{1,0:T(8,128)S(1)}, f32[16,1792]{1,0:T(8,128)S(1)}, u32[]{:S(2)}, u32[]{:S(2)}) collective-permute-start(f32[16,1792]{1,0:T(8,128)S(1)} %fusion), channel_id=1, source_target_pairs={{0,8},{1,9},{2,10},{3,11},{4,12},{5,13},{6,14},{7,15},{8,16},{9,17... | collective-permute-start | bytes 344072
  816.8 1.9 collective-permute-start.8
  818.8 1.9 collective-permute-start.9
  820.9 5.7 collective-permute-done.8
  826.6 0.6 copy-done.23
  827.2 1.7 collective-permute-done.9
  828.9 13.6 %concatenate = f32[270,1792]{1,0:T(8,128)S(1)} concatenate(f32[14,1792]{1,0:T(8,128)S(1)} %collective-permute-done.15, f32[16,1792]{1,0:T(8,128)} %copy-done.16, f32[16,1792]{1,0:T(8,128)} %copy-done.15, f32[16,1792]{1,0:T(8,128)} %copy-done.14, f32[16,1792]{1,0:T(8,128)} %copy-done.13, f32[16,1792]{1,0:T(8,128)} %copy-done.12, f32[16,1792]{1,0:T(8,128)} %collective-permute-done.9, ...), dimensions={0} | concatenate | bytes 3870720
  842.5 0.7 constant_dynamic-slice_fusion
  (83 shorter events, 0.3 us)
Async XLA Ops:
  7.2 1.6 copy-start
  7.2 3.6 copy-start.8
  7.2 96.6 %all-gather.2.cloned.1.call-start = ((), (), s32[]{:S(2)}) async-start(), calls=%async_computation.2 | async-start | bytes 17825792 | tf_op jit(solution)/shard_map/all_gather | solution.py:142
  7.9 224.8 %reduce-scatter.5.cloned.1.call-start = ((), (), s32[]{:S(2)}) async-start(), calls=%async_computation.3 | async-start | bytes 9437184 | tf_op jit(solution)/shard_map/reduce_scatter | solution.py:145
  12.6 2.2 copy-start.25
  14.8 3.4 copy-start.26
  120.6 0.7 copy-start.29
  120.6 112.1 %copy-start.9 = (bf16[8,64,1024]{2,1,0:T(8,128)(2,1)S(1)}, bf16[8,64,1024]{2,1,0:T(8,128)(2,1)}, u32[]{:S(2)}) copy-start(bf16[8,64,1024]{2,1,0:T(8,128)(2,1)} %param.25) | copy-start | bytes 3145732
  120.6 112.1 %copy-start.28 = (f32[1024]{0:T(1024)S(1)}, f32[1024]{0:T(1024)}, u32[]{:S(2)}) copy-start(f32[1024]{0:T(1024)} %param.27) | copy-start | bytes 12292
  120.6 210.1 %reduce-scatter.7.cloned.1.call-start = ((), (), s32[]{:S(2)}) async-start(), calls=%async_computation.4 | async-start | bytes 4128768 | tf_op jit(solution)/shard_map/reduce_scatter | solution.py:158
  246.5 5.1 copy-start.24
  246.5 5.1 copy-start.6
  246.5 5.1 copy-start.7
  246.5 5.1 copy-start.11
  251.6 4.1 copy-start.27
  252.8 2.9 copy-start.2
  267.1 6.1 copy-start.10
  336.0 4.2 copy-start.3
  340.2 8.5 copy-start.5
  355.0 8.9 %copy-start.4 = (f32[1,1024,128]{2,1,0:T(8,128)}, f32[1,1024,128]{2,1,0:T(8,128)S(1)}, u32[]{:S(2)}) copy-start(f32[1,1024,128]{2,1,0:T(8,128)S(1)} %fusion.24) | copy-start | bytes 1572868
  392.6 450.5 %copy-start.1 = (bf16[8,64,1024]{2,1,0:T(8,128)(2,1)S(1)}, bf16[8,64,1024]{2,1,0:T(8,128)(2,1)}, u32[]{:S(2)}) copy-start(bf16[8,64,1024]{2,1,0:T(8,128)(2,1)} %param.21) | copy-start | bytes 3145732
  742.6 9.7 %collective-permute-start.15 = (f32[14,1792]{1,0:T(8,128)S(1)}, f32[14,1792]{1,0:T(8,128)S(1)}, u32[]{:S(2)}, u32[]{:S(2)}) collective-permute-start(f32[14,1792]{1,0:T(8,128)S(1)} %slice.14), channel_id=1, source_target_pairs={{0,16},{1,17},{2,18},{3,19},{4,20},{5,21},{6,22},{7,23},{8,24},{9,... | collective-permute-start | bytes 301064
  743.9 15.0 %collective-permute-start = (f32[16,1792]{1,0:T(8,128)S(1)}, f32[16,1792]{1,0:T(8,128)S(1)}, u32[]{:S(2)}, u32[]{:S(2)}) collective-permute-start(f32[16,1792]{1,0:T(8,128)S(1)} %fusion), channel_id=1, source_target_pairs={{0,1},{1,2},{2,3},{3,4},{4,5},{5,6},{6,7},{7,8},{8,9},{9,10},{10,1... | collective-permute-start | bytes 344072
  745.8 14.4 %collective-permute-start.1 = (f32[16,1792]{1,0:T(8,128)S(1)}, f32[16,1792]{1,0:T(8,128)S(1)}, u32[]{:S(2)}, u32[]{:S(2)}) collective-permute-start(f32[16,1792]{1,0:T(8,128)S(1)} %fusion), channel_id=1, source_target_pairs={{0,2},{1,3},{2,4},{3,5},{4,6},{5,7},{6,8},{7,9},{8,10},{9,11},{10,... | collective-permute-start | bytes 344072
  747.7 30.0 %collective-permute-start.10 = (f32[16,1792]{1,0:T(8,128)S(1)}, f32[16,1792]{1,0:T(8,128)S(1)}, u32[]{:S(2)}, u32[]{:S(2)}) collective-permute-start(f32[16,1792]{1,0:T(8,128)S(1)} %fusion), channel_id=1, source_target_pairs={{0,11},{1,12},{2,13},{3,14},{4,15},{5,16},{6,17},{7,18},{8,19},{9,... | collective-permute-start | bytes 344072
  749.6 30.0 %collective-permute-start.11 = (f32[16,1792]{1,0:T(8,128)S(1)}, f32[16,1792]{1,0:T(8,128)S(1)}, u32[]{:S(2)}, u32[]{:S(2)}) collective-permute-start(f32[16,1792]{1,0:T(8,128)S(1)} %fusion), channel_id=1, source_target_pairs={{0,12},{1,13},{2,14},{3,15},{4,16},{5,17},{6,18},{7,19},{8,20},{9,... | collective-permute-start | bytes 344072
  752.3 30.5 %collective-permute-start.12 = (f32[16,1792]{1,0:T(8,128)S(1)}, f32[16,1792]{1,0:T(8,128)S(1)}, u32[]{:S(2)}, u32[]{:S(2)}) collective-permute-start(f32[16,1792]{1,0:T(8,128)S(1)} %fusion), channel_id=1, source_target_pairs={{0,13},{1,14},{2,15},{3,16},{4,17},{5,18},{6,19},{7,20},{8,21},{9,... | collective-permute-start | bytes 344072
  758.8 27.8 %collective-permute-start.13 = (f32[16,1792]{1,0:T(8,128)S(1)}, f32[16,1792]{1,0:T(8,128)S(1)}, u32[]{:S(2)}, u32[]{:S(2)}) collective-permute-start(f32[16,1792]{1,0:T(8,128)S(1)} %fusion), channel_id=1, source_target_pairs={{0,14},{1,15},{2,16},{3,17},{4,18},{5,19},{6,20},{7,21},{8,22},{9,... | collective-permute-start | bytes 344072
  760.2 29.1 %collective-permute-start.14 = (f32[16,1792]{1,0:T(8,128)S(1)}, f32[16,1792]{1,0:T(8,128)S(1)}, u32[]{:S(2)}, u32[]{:S(2)}) collective-permute-start(f32[16,1792]{1,0:T(8,128)S(1)} %fusion), channel_id=1, source_target_pairs={{0,15},{1,16},{2,17},{3,18},{4,19},{5,20},{6,21},{7,22},{8,23},{9,... | collective-permute-start | bytes 344072
  777.8 41.0 %copy-start.12 = (f32[16,1792]{1,0:T(8,128)}, f32[16,1792]{1,0:T(8,128)S(1)}, u32[]{:S(2)}) copy-start(f32[16,1792]{1,0:T(8,128)S(1)} %collective-permute-done.10) | copy-start | bytes 344068
  777.8 21.4 %collective-permute-start.2 = (f32[16,1792]{1,0:T(8,128)S(1)}, f32[16,1792]{1,0:T(8,128)S(1)}, u32[]{:S(2)}, u32[]{:S(2)}) collective-permute-start(f32[16,1792]{1,0:T(8,128)S(1)} %fusion), channel_id=1, source_target_pairs={{0,3},{1,4},{2,5},{3,6},{4,7},{5,8},{6,9},{7,10},{8,11},{9,12},{10... | collective-permute-start | bytes 344072
  779.7 41.0 %copy-start.13 = (f32[16,1792]{1,0:T(8,128)}, f32[16,1792]{1,0:T(8,128)S(1)}, u32[]{:S(2)}) copy-start(f32[16,1792]{1,0:T(8,128)S(1)} %collective-permute-done.11) | copy-start | bytes 344068
  779.7 37.1 %collective-permute-start.3 = (f32[16,1792]{1,0:T(8,128)S(1)}, f32[16,1792]{1,0:T(8,128)S(1)}, u32[]{:S(2)}, u32[]{:S(2)}) collective-permute-start(f32[16,1792]{1,0:T(8,128)S(1)} %fusion), channel_id=1, source_target_pairs={{0,4},{1,5},{2,6},{3,7},{4,8},{5,9},{6,10},{7,11},{8,12},{9,13},{1... | collective-permute-start | bytes 344072
  782.9 37.9 %copy-start.14 = (f32[16,1792]{1,0:T(8,128)}, f32[16,1792]{1,0:T(8,128)S(1)}, u32[]{:S(2)}) copy-start(f32[16,1792]{1,0:T(8,128)S(1)} %collective-permute-done.12) | copy-start | bytes 344068
  782.9 35.9 %collective-permute-start.4 = (f32[16,1792]{1,0:T(8,128)S(1)}, f32[16,1792]{1,0:T(8,128)S(1)}, u32[]{:S(2)}, u32[]{:S(2)}) collective-permute-start(f32[16,1792]{1,0:T(8,128)S(1)} %fusion), channel_id=1, source_target_pairs={{0,5},{1,6},{2,7},{3,8},{4,9},{5,10},{6,11},{7,12},{8,13},{9,14},{... | collective-permute-start | bytes 344072
  786.7 34.1 %copy-start.15 = (f32[16,1792]{1,0:T(8,128)}, f32[16,1792]{1,0:T(8,128)S(1)}, u32[]{:S(2)}) copy-start(f32[16,1792]{1,0:T(8,128)S(1)} %collective-permute-done.13) | copy-start | bytes 344068
  786.7 34.1 %collective-permute-start.5 = (f32[16,1792]{1,0:T(8,128)S(1)}, f32[16,1792]{1,0:T(8,128)S(1)}, u32[]{:S(2)}, u32[]{:S(2)}) collective-permute-start(f32[16,1792]{1,0:T(8,128)S(1)} %fusion), channel_id=1, source_target_pairs={{0,6},{1,7},{2,8},{3,9},{4,10},{5,11},{6,12},{7,13},{8,14},{9,15},... | collective-permute-start | bytes 344072
  789.3 31.5 %copy-start.16 = (f32[16,1792]{1,0:T(8,128)}, f32[16,1792]{1,0:T(8,128)S(1)}, u32[]{:S(2)}) copy-start(f32[16,1792]{1,0:T(8,128)S(1)} %collective-permute-done.14) | copy-start | bytes 344068
  789.3 31.5 %collective-permute-start.6 = (f32[16,1792]{1,0:T(8,128)S(1)}, f32[16,1792]{1,0:T(8,128)S(1)}, u32[]{:S(2)}, u32[]{:S(2)}) collective-permute-start(f32[16,1792]{1,0:T(8,128)S(1)} %fusion), channel_id=1, source_target_pairs={{0,7},{1,8},{2,9},{3,10},{4,11},{5,12},{6,13},{7,14},{8,15},{9,16}... | collective-permute-start | bytes 344072
  799.2 21.6 %copy-start.17 = (f32[16,1792]{1,0:T(8,128)}, f32[16,1792]{1,0:T(8,128)S(1)}, u32[]{:S(2)}) copy-start(f32[16,1792]{1,0:T(8,128)S(1)} %collective-permute-done.2) | copy-start | bytes 344068
  799.2 21.7 %collective-permute-start.7 = (f32[16,1792]{1,0:T(8,128)S(1)}, f32[16,1792]{1,0:T(8,128)S(1)}, u32[]{:S(2)}, u32[]{:S(2)}) collective-permute-start(f32[16,1792]{1,0:T(8,128)S(1)} %fusion), channel_id=1, source_target_pairs={{0,8},{1,9},{2,10},{3,11},{4,12},{5,13},{6,14},{7,15},{8,16},{9,17... | collective-permute-start | bytes 344072
  816.8 4.0 copy-start.18
  816.8 9.7 %collective-permute-start.8 = (f32[16,1792]{1,0:T(8,128)S(1)}, f32[16,1792]{1,0:T(8,128)S(1)}, u32[]{:S(2)}, u32[]{:S(2)}) collective-permute-start(f32[16,1792]{1,0:T(8,128)S(1)} %fusion), channel_id=1, source_target_pairs={{0,9},{1,10},{2,11},{3,12},{4,13},{5,14},{6,15},{7,16},{8,17},{9,1... | collective-permute-start | bytes 344072
  818.8 2.0 copy-start.19
  818.8 10.1 %collective-permute-start.9 = (f32[16,1792]{1,0:T(8,128)S(1)}, f32[16,1792]{1,0:T(8,128)}, u32[]{:S(2)}, u32[]{:S(2)}) collective-permute-start(f32[16,1792]{1,0:T(8,128)S(1)} %fusion), channel_id=1, source_target_pairs={{0,10},{1,11},{2,12},{3,13},{4,14},{5,15},{6,16},{7,17},{8,18},{9,... | collective-permute-start | bytes 344072
  820.8 5.8 copy-start.20
  820.8 5.7 copy-start.21
  820.8 5.7 copy-start.22
  826.6 0.7 copy-start.23
Sparse Core Ops, SparseCore 0:
  9.7 94.0 all-gather.1
  120.7 111.9 reduce-scatter.4
  251.1 79.6 reduce-scatter.6
where the time goes:
time: 851 us; the launch traced here: 850 us
  blocking collectives  369 us (43%)
  waiting for transfers between devices  248 us (29%)
  matrix products  91.5 us (11%)
  starting transfers between devices  72 us (8%)
  local copies, waits for them, and re-layouts  45.5 us (5%)
  between operations  15.1 us (2%)
  other arithmetic  9.45 us (1%)
    unnamed x1, blocking collectives  350 us
    reduce_scatter x1, waiting for transfers between devices, on_device(): lax.psum_scatter(partial_value, 'tensor', scatter_dimension=1, tiled=True)  111 us
    all_gather x1, waiting for transfers between devices, on_device(): lax.all_gather(out_weight, 'dp', axis=1, tiled=True)  84.1 us
    unnamed x16, starting transfers between devices  71.7 us
    reduce_scatter x1, waiting for transfers between devices, on_device(): lax.psum_scatter(moved, 'tensor', scatter_dimension=0, tiled=True)  37.8 us
    psum x1, blocking collectives, on_device(): totals = lax.psum(moved_squares, 'tensor')  18.6 us
    unnamed x63, local copies, waits for them, and re-layouts  18.3 us
  transfers between devices with their start and end apart: 19, of which 6 were waited for; matrix products, arithmetic and copies ran while one was open for 4% of the time, Pallas kernels for 0%

commit v1 on v0

v1 whole, which is shorter than its diff:
```python
import math

import jax
import jax.numpy as jnp
from jax import lax
from jax.experimental import pallas as pl
from jax.experimental.pallas import tpu as pltpu
from jax.sharding import PartitionSpec as P

D = 8192
HEAD = 128
NQ = 64
DHEAD = 112
NT = 1000
W = 1792
IMG_HEADS = 16
F32 = jnp.float32
BF16 = jnp.bfloat16
MESH = pl.DeviceIdType.MESH

eps = 1e-06
grad_gain = 16.0

ROWS_BLOCK = 14
ROWS_PAD = 16
GRAY = ((0, 3), (1, 2))
PIECES = (384, 384, 256, 256, 256, 256)
STARTS = (0, 384, 768, 1024, 1280, 1536)
KEY_WINDOWS = (0, 384, 896, 1280)
SCORE_WINDOWS = (0, 128, 256, 384, 512, 640, 768)


def nt_dot(a, b):
    return lax.dot_general(a, b, (((1,), (1,)), ((), ())), preferred_element_type=F32)


def nn_dot(a, b):
    return jnp.dot(a, b, preferred_element_type=F32)


def place_of_block(natural):
    z, y_hi = natural % 4, natural // 4 % 2
    core, y_lo, x = natural // 8 % 2, natural // 16 % 2, natural // 32
    place = core
    for i in (x, y_hi * 2 + y_lo, z):
        a, b = (i + i // 2) % 2, i // 2
        place = place * 4 + a * 2 + b
    return place


def head_mask(rows, width, head, base):
    lane = lax.broadcasted_iota(jnp.int32, (rows, width), 1) + base
    return (lane >= head * DHEAD) & (lane < (head + 1) * DHEAD)


def only_head(block, head, base):
    return jnp.where(head_mask(*block.shape, head, base), block.astype(F32), 0.0).astype(BF16)


def step_kernel(
    gain, q_ref, hv_ref, lat_ref, noise_ref, cond_ref, vhw_ref, vel_ref, dq_ref, kbd, kflat, vw, ones, probs, dsc
):
    scale = 1.0 / DHEAD**0.5
    keys = cond_ref.shape[0]

    @pl.when(pl.program_id(0) == 0)
    def _():
        for g, base in enumerate(KEY_WINDOWS):
            vals = []
            for n in range(4):
                window = cond_ref[:, base : base + 512]
                kbd[g, n * keys : (n + 1) * keys, :] = only_head(window, 4 * g + n, base)
                window = cond_ref[:, W + base : W + base + 512]
                vals.append(only_head(window, 4 * g + n, base))
            vw[g] = nn_dot(jnp.concatenate(vals, 0), vhw_ref[base : base + 512, :]).astype(BF16)
        for tile, first in enumerate(SCORE_WINDOWS):
            for n in range(4):
                window = cond_ref[:, tile * 256 : (tile + 1) * 256]
                kflat[tile, n * keys : (n + 1) * keys, :] = only_head(window, first // keys + n, tile * 256)
        row = lax.broadcasted_iota(jnp.int32, (256, 256), 0) // keys
        column = lax.broadcasted_iota(jnp.int32, (256, 256), 1) // keys
        ones[...] = jnp.where(row == column, 1.0, 0.0).astype(BF16)

    velocity = hv_ref[...]
    for g, base in enumerate(KEY_WINDOWS):
        expo = jnp.exp(nt_dot(q_ref[:, base : base + 512], kbd[g]) * scale)
        total = nn_dot(jnp.minimum(expo, 3.38e38).astype(BF16), ones[...])
        p = expo / total
        probs[:, g * 256 : (g + 1) * 256] = p
        velocity = velocity + nn_dot(p.astype(BF16), vw[g])
    vel_ref[...] = velocity
    target = noise_ref[...].astype(F32) - lat_ref[...].astype(F32)
    dvel = ((velocity - target) * gain).astype(BF16)
    for g in range(4):
        p = probs[:, g * 256 : (g + 1) * 256]
        dprob = nt_dot(dvel, vw[g])
        both = p * dprob
        high = both.astype(BF16)
        low = (both - high.astype(F32)).astype(BF16)
        shift = nn_dot(high, ones[...]) + nn_dot(low, ones[...])
        dsc[:, g * 256 : (g + 1) * 256] = (p * (dprob - shift) * scale).astype(BF16)
    for tile, first in enumerate(SCORE_WINDOWS):
        dq_ref[:, tile * 256 : (tile + 1) * 256] = nn_dot(dsc[:, first : first + 256], kflat[tile]).astype(BF16)


def step(q, hv, latents, noise, cond, vhw, gain):
    tokens = q.shape[0]
    block = 256
    keys = cond.shape[0]
    whole = lambda a: pl.BlockSpec(a.shape, lambda i: (0,) * a.ndim)
    rows = lambda width: pl.BlockSpec((block, width), lambda i: (i, 0))
    return pl.pallas_call(
        lambda *refs: step_kernel(gain, *refs),
        grid=(tokens // block,),
        in_specs=[rows(W), rows(128), rows(128), rows(128), whole(cond), whole(vhw)],
        out_specs=[rows(128), rows(W)],
        out_shape=[jax.ShapeDtypeStruct((tokens, 128), F32), jax.ShapeDtypeStruct((tokens, W), BF16)],
        scratch_shapes=[
            pltpu.VMEM((4, 4 * keys, 512), BF16),
            pltpu.VMEM((7, 4 * keys, 256), BF16),
            pltpu.VMEM((4, 4 * keys, 128), BF16),
            pltpu.VMEM((256, 256), BF16),
            pltpu.VMEM((block, 1024), F32),
            pltpu.VMEM((block, 1024), BF16),
        ],
        compiler_params=pltpu.CompilerParams(vmem_limit_bytes=48 << 20),
        cost_estimate=pl.CostEstimate(flops=6 * 10**9, bytes_accessed=10 * 10**6, transcendentals=10**6),
        name="flow_step",
    )(q, hv, latents, noise, cond, vhw)


def places():
    dp, tensor = lax.axis_index("dp"), lax.axis_index("tensor")
    return dp // 4, (tensor // 4) * 2 + (dp // 2) % 2, tensor % 4, dp % 2


def device_at(x, y, z, core):
    return (x * 4 + (y % 2) * 2 + core, (y // 2) * 4 + z)


def link_partners(x, y, z, core):
    pair = lambda i: i + 1 - 2 * (i % 2)
    other = lambda i: 3 - i
    return (
        device_at(pair(x), y, z, core),
        device_at(other(x), y, z, core),
        device_at(x, pair(y), z, core),
        device_at(x, other(y), z, core),
        device_at(x, y, pair(z), core),
        device_at(x, y, other(z), core),
    )


def gray_bits(i):
    return (i + i // 2) % 2, i // 2


def grad_kernel(nt_ref, dq_ref, out_ref, *scratch):
    mine, away, sibling_part = scratch[0:6], scratch[6:12], scratch[12:18]
    landing = [scratch[18 + 6 * p : 24 + 6 * p] for p in range(6)]
    core_send, core_recv, send_sem, recv_sem = scratch[54:58]
    x, y, z, core = places()
    partners = link_partners(x, y, z, core)
    sibling = device_at(x, y, z, 1 - core)
    bits = gray_bits(x) + gray_bits(y) + gray_bits(z)

    barrier = pltpu.get_barrier_semaphore()
    for device in partners + (sibling,):
        pl.semaphore_signal(barrier, inc=1, device_id=device, device_id_type=MESH)
    pl.semaphore_wait(barrier, 7)

    def product(p, which, target):
        columns = pl.ds(STARTS[p], PIECES[p])

        def part(i, carry):
            rows = nt_ref[which, pl.ds(pl.multiple_of(i * 512, 512), 512), :]
            value = nn_dot(rows, dq_ref[:, columns]).astype(BF16)
            target[i] = value.reshape(2, 2, 2, 2, 2, ROWS_PAD, PIECES[p])
            return carry

        lax.fori_loop(0, 2, part, 0)

    def region(p, k, bit):
        index = []
        for dim in range(6):
            age = (dim - p) % 6
            index.append(bits[dim] if age < k else bit if age == k else slice(None))
        return tuple(index)

    def to_sibling(p):
        return pltpu.make_async_remote_copy(
            src_ref=away[p],
            dst_ref=sibling_part[p],
            send_sem=core_send.at[p],
            recv_sem=core_recv.at[p],
            device_id=sibling,
            device_id_type=MESH,
        )

    def exchange(p, k):
        dim = (p + k) % 6
        return pltpu.make_async_remote_copy(
            src_ref=mine[p].at[region(p, k, 1 - bits[dim])],
            dst_ref=landing[p][k],
            send_sem=send_sem.at[p, k],
            recv_sem=recv_sem.at[p, k],
            device_id=partners[dim],
            device_id_type=MESH,
        )

    sent = []
    flying = {}

    def send(p, copy):
        copy.start()
        flying[p] = copy
        sent.append(copy)

    def settle(p, k):
        flying[p].wait_recv()
        if k == 0:
            index = (slice(None),) * 6
            arrived = sibling_part[p]
        else:
            index = region(p, k - 1, bits[(p + k - 1) % 6])
            arrived = landing[p][k - 1]
        total = mine[p][index].astype(F32) + arrived[...].astype(F32)
        if k == 6:
            out_ref[:, STARTS[p] : STARTS[p] + PIECES[p]] = total
        else:
            mine[p][index] = total.astype(BF16)
            send(p, exchange(p, k))

    for p in range(7):
        if p < 6:
            product(p, 1 - core, away[p])
            send(p, to_sibling(p))
            product(p, core, mine[p])
        if p > 0:
            settle(p - 1, 0)
    for k in range(1, 7):
        for p in range(6):
            settle(p, k)
    for copy in sent:
        copy.wait_send()


def summed_gradient(normed_t, dq):
    tokens = dq.shape[0]
    full = [pltpu.VMEM((2,) * 6 + (ROWS_PAD, c), BF16) for c in PIECES]
    parts = [pltpu.VMEM((2,) * (5 - k) + (ROWS_PAD, c), BF16) for c in PIECES for k in range(6)]
    out = pl.pallas_call(
        grad_kernel,
        out_shape=jax.ShapeDtypeStruct((ROWS_PAD, W), F32),
        in_specs=[pl.BlockSpec(memory_space=pltpu.VMEM)] * 2,
        out_specs=pl.BlockSpec(memory_space=pltpu.VMEM),
        scratch_shapes=full
        + full
        + full
        + parts
        + [
            pltpu.SemaphoreType.DMA((6,)),
            pltpu.SemaphoreType.DMA((6,)),
            pltpu.SemaphoreType.DMA((6, 6)),
            pltpu.SemaphoreType.DMA((6, 6)),
        ],
        compiler_params=pltpu.CompilerParams(
            collective_id=1, has_side_effects=True, vmem_limit_bytes=48 << 20
        ),
        name="grad_sum",
    )(normed_t.reshape(2, -1, tokens), dq)
    return out[:ROWS_BLOCK]


def attend(m, owner_ref, len_ref, q_ref, pk_ref, pv_ref, ok_ref, ov_ref, att):
    prompt = owner_ref[0, m]
    length = len_ref[prompt]
    scale = 1.0 / HEAD**0.5
    own_k, own_v = ok_ref[prompt], ov_ref[prompt]
    keys, values = pk_ref[prompt], pv_ref[prompt]
    states = q_ref[prompt]
    heads = states.shape[1] // HEAD
    rows = jnp.concatenate([states[:, j * HEAD : (j + 1) * HEAD] for j in range(heads)], 0)
    first = nt_dot(rows, keys) * scale
    second = nt_dot(rows, own_k) * scale
    column = lax.broadcasted_iota(jnp.int32, first.shape, 1)
    first = jnp.where(column < length, first, -jnp.inf)
    row = lax.broadcasted_iota(jnp.int32, second.shape, 0) % NQ
    column = lax.broadcasted_iota(jnp.int32, second.shape, 1)
    second = jnp.where(column <= row, second, -jnp.inf)
    top = jnp.maximum(jnp.max(first, -1, keepdims=True), jnp.max(second, -1, keepdims=True))
    first, second = jnp.exp(first - top), jnp.exp(second - top)
    total = jnp.sum(first, -1, keepdims=True) + jnp.sum(second, -1, keepdims=True)
    out = nn_dot(first.astype(BF16), values) + nn_dot(second.astype(BF16), own_v)
    out = (out / total).astype(BF16)
    rows_at = pl.ds(pl.multiple_of(m * NQ, NQ), NQ)
    for j in range(heads):
        att[rows_at, j * HEAD : (j + 1) * HEAD] = out[j * NQ : (j + 1) * NQ]


def greet(devices):
    barrier = pltpu.get_barrier_semaphore()
    for device in devices:
        pl.semaphore_signal(barrier, inc=1, device_id=device, device_id_type=MESH)
    pl.semaphore_wait(barrier, len(devices))


def project_kernel(
    owner_ref,
    len_ref,
    q_ref,
    pk_ref,
    pv_ref,
    ok_ref,
    ov_ref,
    res_ref,
    w_ref,
    gain_ref,
    scaled_ref,
    sq_ref,
    att,
    wg,
    terms,
    land1,
    land2,
    zsum,
    landy,
    own_sem,
    w_send,
    w_recv,
    r_send,
    r_recv,
    y_send,
    y_recv,
):
    x, y, z, core = places()
    y_lo, y_hi = y % 2, y // 2
    xp, xo, xf = x + 1 - 2 * (x % 2), 3 - x, (x + 2) % 4
    at_y = device_at(x, y + 1 - 2 * y_lo, z, core)
    at_xp, at_xo = device_at(xp, y, z, core), device_at(xo, y, z, core)
    at_ze, at_zo = device_at(x, y, z + 1 - 2 * (z % 2), core), device_at(x, y, 3 - z, core)
    at_far = device_at(x, (y + 2) % 4, z, core)
    at_sib = device_at(x, y, z, 1 - core)
    bit_a, bit_b = gray_bits(z)
    sent, shared = [], []

    greet((at_y, at_xp, at_xo, at_ze, at_zo, at_far, at_sib))

    def share(xs, ys, h, target, own=False):
        slot = wg.at[xs, ys, core, h]
        number = len(shared)
        shared.append(target)
        copy = pltpu.make_async_remote_copy(
            src_ref=w_ref.at[:, h * 256 : (h + 1) * 256] if own else slot,
            dst_ref=slot,
            send_sem=w_send.at[number],
            recv_sem=w_recv.at[xs, ys, core, h],
            device_id=target,
            device_id_type=MESH,
        )
        copy.start()
        sent.append(copy)

    def arrived(xs, ys, cs, h):
        slot = wg.at[xs, ys, cs, h]
        pltpu.make_async_remote_copy(
            src_ref=slot,
            dst_ref=slot,
            send_sem=w_send.at[0],
            recv_sem=w_recv.at[xs, ys, cs, h],
            device_id=at_sib,
            device_id_type=MESH,
        ).wait_recv()

    def pass_on(xs, ys, h, *targets):
        arrived(xs, ys, core, h)
        for target in targets:
            share(xs, ys, h, target)

    keep = [
        pltpu.make_async_copy(w_ref.at[:, h * 256 : (h + 1) * 256], wg.at[x, y_lo, core, h], own_sem.at[h])
        for h in range(2)
    ]
    for h in range(2):
        for target in (at_xp, at_y, at_xo, at_sib):
            share(x, y_lo, h, target, own=True)
        keep[h].start()

    def prompts(start, end):
        def body(m, carry):
            attend(m, owner_ref, len_ref, q_ref, pk_ref, pv_ref, ok_ref, ov_ref, att)
            return carry

        lax.fori_loop(start, end, body, 0)

    prompts(0, 4)
    pass_on(x, 1 - y_lo, 0, at_xp, at_xo, at_sib)
    pass_on(xp, y_lo, 0, at_sib)
    pass_on(xo, y_lo, 0, at_xp, at_sib)
    prompts(4, 8)
    pass_on(x, 1 - y_lo, 1, at_xp, at_xo, at_sib)
    pass_on(xp, y_lo, 1, at_xo, at_sib)
    pass_on(xo, y_lo, 1, at_sib)
    for copy in keep:
        copy.wait()

    def reduce_copy(s, part, phase):
        block = terms.at[s, part]
        if phase == 0:
            source = block.at[1 - bit_a] if part == 0 else block.at[:, 1 - bit_b]
            landing = land1.at[s, part]
        else:
            source = block.at[bit_a, 1 - bit_b] if part == 0 else block.at[1 - bit_a, bit_b]
            landing = land2.at[s, part]
        return pltpu.make_async_remote_copy(
            src_ref=source,
            dst_ref=landing,
            send_sem=r_send.at[s, part, phase],
            recv_sem=r_recv.at[s, part, phase],
            device_id=at_ze if part == phase else at_zo,
            device_id_type=MESH,
        )

    flying = {}

    def launch(key, copy):
        copy.start()
        sent.append(copy)
        flying[key] = copy

    def multiply(s, half, cs, h):
        def body(i, carry):
            u, v = i // 2, i % 2
            value = nn_dot(att[...], wg[2 * half + u, v, cs, h]).astype(BF16)
            a, b = (u + v) % 2, u
            terms[s, 0, a, b] = value[:256]
            terms[s, 1, a, b] = value[256:]
            return carry

        lax.fori_loop(0, 4, body, 0)
        for part in range(2):
            launch((s, part), reduce_copy(s, part, 0))

    def halve(s):
        for part in range(2):
            flying[s, part].wait_recv()
            index = (s, 0, bit_a) if part == 0 else (s, 1, slice(None), bit_b)
            total = terms[index].astype(F32) + land1[s, part].astype(F32)
            terms[index] = total.astype(BF16)
            launch((s, part), reduce_copy(s, part, 1))

    def finish(s, half):
        for part in range(2):
            flying[s, part].wait_recv()
            total = terms[s, part, bit_a, bit_b].astype(F32) + land2[s, part].astype(F32)
            zsum[half, s % 4, part * 256 : (part + 1) * 256] = total.astype(BF16)
        if s >= 4:
            i = s - 4
            launch(
                ("y", i),
                pltpu.make_async_remote_copy(
                    src_ref=zsum.at[1 - y_hi, i],
                    dst_ref=landy.at[i],
                    send_sem=y_send.at[i],
                    recv_sem=y_recv.at[i],
                    device_id=at_far,
                    device_id_type=MESH,
                ),
            )

    def close(i, cs, h):
        flying["y", i].wait_recv()
        columns = pl.ds(pl.multiple_of(cs * 512 + h * 256, 256), 256)
        gain = gain_ref[:, columns]

        def body(m, carry):
            rows = pl.ds(pl.multiple_of(m * NQ, NQ), NQ)
            value = res_ref[owner_ref[0, m], :, columns].astype(F32)
            value = value + (zsum[y_hi, i, rows, :].astype(F32) + landy[i, rows, :].astype(F32))
            scaled_ref[rows, columns] = (value * gain).astype(BF16)
            square = value * value
            square = square[:, :128] + square[:, 128:]
            sq_ref[rows, :] = square if i == 0 else sq_ref[rows, :] + square
            return carry

        lax.fori_loop(0, 8, body, 0)

    halves = (x // 2, 1 - x // 2)
    order = [(halves[s // 4], (core, 1 - core)[s % 2], s // 2 % 2) for s in range(8)]
    for s in range(8):
        half, cs, h = order[s]
        if s == 0:
            pass_on(xp, 1 - y_lo, 0, at_sib)
        if s == 1:
            for xs in (x, xp):
                for ys in (y_lo, 1 - y_lo):
                    arrived(xs, ys, 1 - core, 0)
        if s == 2:
            pass_on(xp, 1 - y_lo, 1, at_sib)
            pass_on(xf, y_lo, 0, at_y, at_sib)
            pass_on(xf, y_lo, 1, at_y, at_sib)
        if s == 3:
            for xs in (x, xp):
                for ys in (y_lo, 1 - y_lo):
                    arrived(xs, ys, 1 - core, 1)
            pass_on(xo, 1 - y_lo, 0, at_sib)
            pass_on(xo, 1 - y_lo, 1, at_sib)
        if s in (4, 6):
            pass_on(xf, 1 - y_lo, s // 2 - 2, at_sib)
        if s in (5, 7):
            for xs in (xo, xf):
                for ys in (y_lo, 1 - y_lo):
                    arrived(xs, ys, 1 - core, s // 2 - 2)
        multiply(s, half, cs, h)
        if s >= 2:
            halve(s - 2)
        if s >= 4:
            finish(s - 4, order[s - 4][0])
    halve(6)
    finish(4, order[4][0])
    halve(7)
    for s in range(5, 8):
        finish(s, order[s][0])
        close(s - 5, *order[s - 1][1:])
    close(3, *order[7][1:])
    for copy in sent:
        copy.wait_send()


def projected(owner, lengths, query_states, prompt_keys, prompt_values, query_keys, query_values, residual, weight, gain):
    rows = query_states.shape[0] * NQ
    vmem, smem = pl.BlockSpec(memory_space=pltpu.VMEM), pl.BlockSpec(memory_space=pltpu.SMEM)
    return pl.pallas_call(
        project_kernel,
        out_shape=[jax.ShapeDtypeStruct((rows, 1024), BF16), jax.ShapeDtypeStruct((rows, 128), F32)],
        in_specs=[smem, smem] + [vmem] * 8,
        out_specs=[vmem] * 2,
        scratch_shapes=[
            pltpu.VMEM((rows, 1024), BF16),
            pltpu.VMEM((4, 2, 2, 2, 1024, 256), BF16),
            pltpu.VMEM((8, 2, 2, 2, 256, 256), BF16),
            pltpu.VMEM((8, 2, 2, 256, 256), BF16),
            pltpu.VMEM((8, 2, 256, 256), BF16),
            pltpu.VMEM((2, 4, rows, 256), BF16),
            pltpu.VMEM((4, rows, 256), BF16),
            pltpu.SemaphoreType.DMA((2,)),
            pltpu.SemaphoreType.DMA((32,)),
            pltpu.SemaphoreType.DMA((4, 2, 2, 2)),
            pltpu.SemaphoreType.DMA((8, 2, 2)),
            pltpu.SemaphoreType.DMA((8, 2, 2)),
            pltpu.SemaphoreType.DMA((4,)),
            pltpu.SemaphoreType.DMA((4,)),
        ],
        compiler_params=pltpu.CompilerParams(
            collective_id=2, has_side_effects=True, vmem_limit_bytes=58 << 20
        ),
        name="attend_project",
    )(
        owner,
        lengths,
        query_states,
        prompt_keys,
        prompt_values,
        query_keys,
        query_values,
        residual,
        weight,
        gain.reshape(1, -1),
    )


COLUMNS = 256
CHUNKS = 2 * W // COLUMNS
TOKENS = 256


def connect_kernel(
    step_ref,
    scaled_ref,
    sq_ref,
    lat_ref,
    noise_ref,
    pw_ref,
    vec_ref,
    vhw_ref,
    pwt_ref,
    col_ref,
    conn_hbm,
    qm_hbm,
    cond_ref,
    hv_ref,
    q_hbm,
    nt_hbm,
    conn,
    qm,
    q_out,
    nt_out,
    buf,
    land1,
    land2,
    land3,
    sqb,
    sq1,
    sq2,
    sq3,
    load_sem,
    out_sem,
    send_sem,
    recv_sem,
):
    x, y, z, core = places()
    y_hi = y // 2
    at_ze, at_zo = device_at(x, y, z + 1 - 2 * (z % 2), core), device_at(x, y, 3 - z, core)
    at_far = device_at(x, (y + 2) % 4, z, core)
    bit_a, bit_b = gray_bits(z)
    loads = [
        pltpu.make_async_copy(
            conn_hbm.at[:, part * 512 : (part + 1) * 512], conn.at[:, part * 512 : (part + 1) * 512], load_sem.at[part]
        )
        for part in range(7)
    ]
    loads.append(pltpu.make_async_copy(qm_hbm, qm, load_sem.at[7]))
    for copy in loads:
        copy.start()

    greet((at_ze, at_zo, at_far))

    sent = []
    flying = {}

    def send(j, phase):
        if j == CHUNKS:
            block, landing = sqb, (sq1, sq2, sq3)[phase]
        else:
            block, landing = buf.at[j], (land1, land2, land3)[phase].at[j]
        if phase == 0:
            source = block.at[:, 1 - bit_a] if j % 2 == 0 else block.at[:, :, 1 - bit_b]
        elif phase == 1:
            source = block.at[:, bit_a, 1 - bit_b] if j % 2 == 0 else block.at[:, 1 - bit_a, bit_b]
        else:
            source = block.at[1 - y_hi, bit_a, bit_b]
        copy = pltpu.make_async_remote_copy(
            src_ref=source,
            dst_ref=landing,
            send_sem=send_sem.at[j, phase],
            recv_sem=recv_sem.at[j, phase],
            device_id=at_far if phase == 2 else at_ze if phase == j % 2 else at_zo,
            device_id_type=MESH,
        )
        copy.start()
        sent.append(copy)
        flying[j] = copy

    def settle(j, phase):
        flying[j].wait_recv()
        if phase == 0:
            index = (slice(None), bit_a) if j % 2 == 0 else (slice(None), slice(None), bit_b)
        else:
            index = (slice(None), bit_a, bit_b)
        if j == CHUNKS:
            sqb[index] = sqb[index] + (sq1, sq2)[phase][...]
        else:
            index = (j,) + index
            total = buf[index].astype(F32) + (land1, land2)[phase][j].astype(F32)
            buf[index] = total.astype(BF16)
        send(j, phase + 1)

    def prelude(c):
        t = (step_ref[0].astype(F32) + 0.5) / NT
        rows = pl.ds(c * TOKENS, TOKENS)
        noisy = ((1.0 - t) * lat_ref[rows, :].astype(F32) + t * noise_ref[rows, :].astype(F32)).astype(BF16)
        hidden = nn_dot(noisy, pw_ref[...]) + t * vec_ref[0:1, :]
        scale = lax.rsqrt(jnp.mean(hidden * hidden, -1, keepdims=True) + eps)
        normed = (hidden * scale * vec_ref[1:2, :]).astype(BF16)
        hv_ref[rows, :] = nn_dot(hidden.astype(BF16), vhw_ref[...])
        q_out[c] = nn_dot(normed, qm[...]).astype(BF16)
        ht = nt_dot(pwt_ref[...], noisy) + t * col_ref[:, 0:1]
        scale_t = lax.rsqrt(jnp.sum(ht * ht, 0, keepdims=True) / W + eps)
        normed_t = (ht * scale_t * col_ref[:, 1:2]).astype(BF16)
        for natural in range(128):
            place = place_of_block(natural) * ROWS_PAD
            nt_out[c, place : place + ROWS_PAD, :] = normed_t[natural * ROWS_PAD : (natural + 1) * ROWS_PAD]
        copies = (
            pltpu.make_async_copy(q_out.at[c], q_hbm.at[c * TOKENS : (c + 1) * TOKENS, :], out_sem.at[c, 0]),
            pltpu.make_async_copy(nt_out.at[c], nt_hbm.at[:, c * TOKENS : (c + 1) * TOKENS], out_sem.at[c, 1]),
        )
        for copy in copies:
            copy.start()
        return copies

    def spread(block, value):
        for m in range(8):
            a, b = gray_bits(m % 4)
            block[m // 4, a, b] = value[m * NQ : (m + 1) * NQ]

    spread(sqb, sq_ref[...])
    send(CHUNKS, 0)
    for j in range(CHUNKS):
        if j % 2 == 0:
            loads[j // 2].wait()
        value = nn_dot(scaled_ref[...], conn[:, j * COLUMNS : (j + 1) * COLUMNS])
        spread(buf.at[j], value.astype(BF16))
        send(j, 0)
    loads[7].wait()
    stores = []
    chunks = [CHUNKS] + list(range(CHUNKS))
    for c in range(4):
        stores += prelude(c)
        for j in chunks[4 * c : 4 * c + 4]:
            settle(j, 0)
        for j in chunks[max(4 * c - 4, 0) : 4 * c]:
            settle(j, 1)
    for j in chunks[12:]:
        settle(j, 1)
    flying[CHUNKS].wait_recv()
    squares = sqb[y_hi, bit_a, bit_b] + sq3[...]
    factor = lax.rsqrt(jnp.sum(squares, -1, keepdims=True) / D + eps)
    for j in range(CHUNKS):
        flying[j].wait_recv()
        total = buf[j, y_hi, bit_a, bit_b].astype(F32) + land3[j].astype(F32)
        cond_ref[:, j * COLUMNS : (j + 1) * COLUMNS] = (total * factor).astype(BF16)
    for copy in stores:
        copy.wait()
    for copy in sent:
        copy.wait_send()


def connected(
    timesteps, scaled, squares, latents, noise, patch_weight, time_embedding, image_norm_gain, vhw, conn_weight, qm
):
    tokens = latents.shape[0]
    blocks = W // ROWS_BLOCK
    pad = ((0, 0), (0, ROWS_PAD - ROWS_BLOCK), (0, 0))
    pwt = jnp.pad(patch_weight.T.reshape(blocks, ROWS_BLOCK, -1), pad).reshape(blocks * ROWS_PAD, -1)
    vec = jnp.stack([time_embedding, image_norm_gain])
    col = jnp.pad(vec.T.reshape(blocks, ROWS_BLOCK, 2), pad).reshape(blocks * ROWS_PAD, 2)
    vmem, smem = pl.BlockSpec(memory_space=pltpu.VMEM), pl.BlockSpec(memory_space=pltpu.SMEM)
    anywhere = pl.BlockSpec(memory_space=pl.ANY)
    return pl.pallas_call(
        connect_kernel,
        out_shape=[
            jax.ShapeDtypeStruct((NQ, 2 * W), BF16),
            jax.ShapeDtypeStruct((tokens, 128), F32),
            jax.ShapeDtypeStruct((tokens, W), BF16),
            jax.ShapeDtypeStruct((blocks * ROWS_PAD, tokens), BF16),
        ],
        in_specs=[smem] + [vmem] * 9 + [anywhere] * 2,
        out_specs=[vmem, vmem, anywhere, anywhere],
        scratch_shapes=[
            pltpu.VMEM(conn_weight.shape, BF16),
            pltpu.VMEM(qm.shape, BF16),
            pltpu.VMEM((4, TOKENS, W), BF16),
            pltpu.VMEM((4, blocks * ROWS_PAD, TOKENS), BF16),
            pltpu.VMEM((CHUNKS, 2, 2, 2, NQ, COLUMNS), BF16),
            pltpu.VMEM((CHUNKS, 2, 2, NQ, COLUMNS), BF16),
            pltpu.VMEM((CHUNKS, 2, NQ, COLUMNS), BF16),
            pltpu.VMEM((CHUNKS, NQ, COLUMNS), BF16),
            pltpu.VMEM((2, 2, 2, NQ, 128), F32),
            pltpu.VMEM((2, 2, NQ, 128), F32),
            pltpu.VMEM((2, NQ, 128), F32),
            pltpu.VMEM((NQ, 128), F32),
            pltpu.SemaphoreType.DMA((8,)),
            pltpu.SemaphoreType.DMA((4, 2)),
            pltpu.SemaphoreType.DMA((CHUNKS + 1, 3)),
            pltpu.SemaphoreType.DMA((CHUNKS + 1, 3)),
        ],
        compiler_params=pltpu.CompilerParams(
            collective_id=3, has_side_effects=True, vmem_limit_bytes=58 << 20
        ),
        name="connect_prelude",
    )(timesteps, scaled, squares, latents, noise, patch_weight, vec, vhw, pwt, col, conn_weight, qm)


def on_device(
    prompt_keys,
    prompt_values,
    query_states,
    query_keys,
    query_values,
    lengths,
    residual,
    out_weight,
    final_gain,
    conn_weight,
    owner,
    latents,
    noise,
    timesteps,
    patch_weight,
    time_embedding,
    image_norm_gain,
    query_matrix,
    velocity_head_weight,
):
    count_of_rows = lax.axis_size("dp") * lax.axis_size("tensor") * latents.shape[1]
    scaled, squares = projected(
        owner,
        lengths,
        query_states,
        prompt_keys,
        prompt_values,
        query_keys,
        query_values,
        residual,
        out_weight,
        final_gain,
    )
    cond, hv, q, normed_t = connected(
        timesteps,
        scaled,
        squares,
        latents[0],
        noise[0],
        patch_weight,
        time_embedding,
        image_norm_gain,
        velocity_head_weight,
        conn_weight,
        query_matrix,
    )
    velocity, dq = step(
        q, hv, latents[0], noise[0], cond, velocity_head_weight, grad_gain / math.sqrt(count_of_rows)
    )
    return (velocity[None], summed_gradient(normed_t, dq))


def solution(mesh):
    return jax.shard_map(
        on_device,
        mesh=mesh,
        in_specs=(
            P("dp", None, "tensor"),
            P("dp", None, "tensor"),
            P("dp", None, "tensor"),
            P("dp", None, "tensor"),
            P("dp", None, "tensor"),
            P("dp"),
            P("dp", None, "tensor"),
            P("tensor", "dp"),
            P("tensor"),
            P("tensor", None),
            P("dp", None),
            P(("dp", "tensor"), None, None),
            P(("dp", "tensor"), None, None),
            P(("dp", "tensor")),
            P(),
            P(),
            P(),
            P(),
            P(),
        ),
        out_specs=(P(("dp", "tensor"), None, None), P(("dp", "tensor"), None)),
        check_vma=False,
    )
```

time: 851 us -> 254 us (0.30)
  blocking collectives: 369 us -> 0 us
  waiting for transfers between devices: 248 us -> 0 us
  Pallas kernels: 0 us -> 238 us
  matrix products: 91.5 us -> 0 us
  starting transfers between devices: 72 us -> 0 us
  local copies, waits for them, and re-layouts: 45.5 us -> 8.53 us
  between operations: 15.1 us -> 1.39 us
  other arithmetic: 9.45 us -> 0.62 us
    unnamed x1 -> x0, blocking collectives: 350 us -> none
    pallas_call x0 -> x4, Pallas kernels: none -> 238 us  [the longest x1 137 us: projected(): pl.pallas_call(project_kernel, out_shape=[jax.ShapeDtypeStruct((rows, 102...]
    reduce_scatter x2 -> x0, waiting for transfers between devices: 149 us -> none  [the longest x1 111 us: on_device(): lax.psum_scatter(partial_value, 'tensor', scatter_dimension=1, tiled=True)]
    dot_general x15 -> x0, matrix products: 91.5 us -> none  [the longest x1 16.8 us: on_device(): jnp.dot(attended, lax.all_gather(out_weight, 'dp', axis=1, tiled=True), p...]
    all_gather x1 -> x0, waiting for transfers between devices: 84.1 us -> none  [on_device(): lax.all_gather(out_weight, 'dp', axis=1, tiled=True)]
    unnamed x16 -> x0, starting transfers between devices: 71.7 us -> none
    convert_element_type x4 -> x0, local copies, waits for them, and re-layouts: 21.2 us -> none  [the longest x1 8.49 us: flow_matching_step(): mixed = (hidden + attn.astype(jnp.float32)).astype(jnp.bfloat16)]
    psum x1 -> x0, blocking collectives: 18.6 us -> none  [on_device(): totals = lax.psum(moved_squares, 'tensor')]
  transfers between devices with their start and end apart: 19 -> 0, of which waited for: 6 -> 0; matrix products, arithmetic and copies ran while one was open for 4% -> 0% of each run, Pallas kernels for 0% -> 0%
where the time goes in v1:
time: 254 us; the launch traced here: 249 us
  Pallas kernels  238 us (94%)
  local copies, waits for them, and re-layouts  8.53 us (3%)
    pallas_call x1, Pallas kernels, projected(): pl.pallas_call(project_kernel, out_shape=[jax.ShapeDtypeStruct((rows, 102...  137 us
    pallas_call x1, Pallas kernels, summed_gradient(): pl.pallas_call(grad_kernel, out_shape=jax.ShapeDtypeStruct((ROWS_PAD, W),...  48 us
    pallas_call x1, Pallas kernels, connected(): pl.pallas_call(connect_kernel, out_shape=[jax.ShapeDtypeStruct((NQ, 2 * W...  42.8 us
    pallas_call x1, Pallas kernels, step(): pl.pallas_call(lambda *refs: step_kernel(gain, *refs), grid=(tokens // bl...  10.7 us

profile of v1, /device:TPU:17, one launch (start us, length us, event | category | flops | bytes accessed | tf_op | source)
XLA Modules:
  0.0 248.7 jit_solution(5491234150842409360)
XLA Ops:
  1.3 0.7 stack.9
  2.0 0.7 stack.10
  2.7 0.6 fusion
  3.3 0.1 reshape.25
  3.5 1.3 copy.23
  4.7 0.1 reshape.23
  4.9 0.9 pad.8
  5.8 0.9 copy.25
  6.7 1.1 pad.9.clone
  7.7 136.7 %attend_project.1 = (bf16[512,1024]{1,0:T(8,128)(2,1)}, f32[512,128]{1,0:T(8,128)}) custom-call(s32[1,8]{1,0:T(1,128)} %owner_ref.1, s32[8]{0:T(128)} %len_ref.1, bf16[8,64,1024]{2,1,0:T(8,128)(2,1)} %q_ref.1, bf16[8,512,128]{2,1,0:T(8,128)(2,1)} %pk_ref.1, bf16[8,512,128]{2,1,0:T(8,128)(2,1)} %pv_ref.1, bf16[8,64,128]{2,1,0:T(8,128)(2,1)} %ok_ref.1, ...), custom_call_target="tpu_custom_call" | custom-call | tf_op jit(solution)/shard_map/attend_project/pallas_call | solution.py:533
  144.4 0.0 copy-start
  144.4 0.0 copy-start.1
  144.4 0.0 copy-start.2
  144.5 42.8 %connect_prelude.1 = (bf16[64,3584]{1,0:T(8,128)(2,1)}, f32[1024,128]{1,0:T(8,128)}, bf16[1024,1792]{1,0:T(8,128)(2,1)}, bf16[2048,1024]{1,0:T(8,128)(2,1)}) custom-call(s32[1]{0:T(128)S(6)} %copy.27.step_ref, bf16[512,1024]{1,0:T(8,128)(2,1)} %get-tuple-element.10.scaled_ref, f32[512,128]{1,0:T(8,128)} %get-tuple-element.11.sq_ref, ...), custom_call_target="tpu_custom_call" | custom-call | tf_op jit(solution)/shard_map/connect_prelude/pallas_call | solution.py:739
  187.2 0.0 copy-done
  187.2 0.0 copy-done.1
  187.2 0.0 copy-done.2
  187.3 0.0 copy-start.3
  187.3 1.0 copy-done.3
  188.3 0.0 copy-start.4
  188.3 1.0 copy-done.4
  189.3 10.7 %flow_step.1 = (f32[1024,128]{1,0:T(8,128)}, bf16[1024,1792]{1,0:T(8,128)(2,1)S(1)}) custom-call(bf16[1024,1792]{1,0:T(8,128)(2,1)} %get-tuple-element.12.refs_0_, f32[1024,128]{1,0:T(8,128)S(1)} %copy-done.3, bf16[1024,128]{1,0:T(8,128)(2,1)S(1)} %bitcast.15, bf16[1024,128]{1,0:T(8,128)(2,1)S(1)} %bitcast.17, bf16[64,3584]{1,0:T(8,128)(2,1)S(1)} %copy-done.4, ...), custom_call_target="tpu_custom_call" | custom-call | flops 6000000000 | bytes 10000000 | tf_op jit(solution)/shard_map/flow_step/pallas_call | solution.py:112
  200.0 48.0 %grad_sum.1 = f32[16,1792]{1,0:T(8,128)S(1)} custom-call(bf16[2,1024,1024]{2,1,0:T(8,128)(2,1)} %bitcast.19, bf16[1024,1792]{1,0:T(8,128)(2,1)S(1)} %get-tuple-element.17.dq_ref), custom_call_target="tpu_custom_call" | custom-call | tf_op jit(solution)/shard_map/grad_sum/pallas_call | solution.py:252
  248.1 0.6 copy.28
Async XLA Ops:
  144.4 42.8 %copy-start = (bf16[1792,128]{1,0:T(8,128)(2,1)S(1)}, bf16[1792,128]{1,0:T(8,128)(2,1)}, u32[]{:S(2)}) copy-start(bf16[1792,128]{1,0:T(8,128)(2,1)} %refs_5_.1) | copy-start | bytes 1376260
  144.4 42.8 %copy-start.1 = (bf16[1,1024,128]{2,1,0:T(8,128)(2,1)S(1)}, bf16[1,1024,128]{2,1,0:T(8,128)(2,1)}, u32[]{:S(2)}) copy-start(bf16[1,1024,128]{2,1,0:T(8,128)(2,1)} %param.30) | copy-start | bytes 786436
  144.4 42.8 %copy-start.2 = (bf16[1,1024,128]{2,1,0:T(8,128)(2,1)S(1)}, bf16[1,1024,128]{2,1,0:T(8,128)(2,1)}, u32[]{:S(2)}) copy-start(bf16[1,1024,128]{2,1,0:T(8,128)(2,1)} %param.31) | copy-start | bytes 786436
  187.3 1.0 copy-start.3
  188.3 1.0 copy-start.4
